TPU v7x, 32 devices: a whole 2x2x4 slice. The times are simulated.
32 devices in a mesh: gx: 4 (over x, core), gy: 8 (over z, y).
Axes of the slice: x: 2, y: 2, z: 4, core: 2. Of those that a mesh axis runs over, the one named last changes fastest.
Arguments:
- views: bfloat16 [384, 49, 2048], P(('gx', 'gy')), may hold values from -6 to 6
- counts: int32 [32], P(('gx', 'gy')), may hold values from 1 to 12, as said below
- partners: int32 [384, 2], P(('gx', 'gy')), may hold values from 0 to 383, as said below
- w_in: bfloat16 [2048, 512], P('gx', 'gy'), may hold values from -0.125 to 0.125
- w_mid: bfloat16 [4608, 512], P('gx', 'gy'), may hold values from -0.09375 to 0.09375
- w_out: bfloat16 [512, 2048], P('gx', 'gy'), may hold values from -0.25 to 0.25
- norm_params: bfloat16 [6144], P(('gx', 'gy')), may hold values from 0.5 to 1.5
Outputs:
- loss_value: float32 [], replicated
- views_grad: float32 [384, 49, 2048], P(('gx', 'gy'))
- w_in_grad: float32 [2048, 512], P('gx', 'gy')
- w_mid_grad: float32 [4608, 512], P('gx', 'gy')
- w_out_grad: float32 [512, 2048], P('gx', 'gy')
- norm_grad: float32 [6144], P(('gx', 'gy'))
Inputs may be any that keep to these rules, and one draw needn't show every extreme that they name: A device's views fill its first counts slots; in every draw some device has all 12 slots filled and some device holds one view. Every entry names a filled slot; a filled slot never lists itself, and its partners lie mostly on other devices. Entries of empty slots are filled slots too.
All inputs are finite; a program needn't handle non-finite values.
Results may differ from a plain program's by a relative error of at most 0.017.
Values may be sent and summed in bfloat16 or wider, within the bound.
No kernel may reach another device: no remote copies, remote signals or barrier semaphores. Data moves between devices by JAX's collectives and lax.ppermute only.
A program may use at most 192 MiB of HBM per device.

v0:
```python
import jax
import jax.numpy as jnp
from jax import lax
from jax.sharding import PartitionSpec as P

SIDE = 7


def collect(w_in, w_mid, w_out, norm_params):
    part_in, part_mid, part_out, part_norm = (
        lax.all_gather(w_in, "gy", axis=1, tiled=True),
        lax.all_gather(w_mid, "gy", axis=1, tiled=True),
        lax.all_gather(w_out, "gy", axis=1, tiled=True),
        lax.all_gather(norm_params, "gy", axis=0, tiled=True),
    )
    return (
        lax.all_gather(part_in, "gx", axis=0, tiled=True),
        lax.all_gather(part_mid, "gx", axis=0, tiled=True),
        lax.all_gather(part_out, "gx", axis=0, tiled=True),
        lax.all_gather(part_norm, "gx", axis=0, tiled=True),
    )


def silu_slope(value):
    sigma = jax.nn.sigmoid(value)
    return sigma * (1.0 + value * (1.0 - sigma))


def normalize(hidden, gain, shift, pixel_weight):
    running, squares, number = lax.psum(
        (
            jnp.sum(hidden * pixel_weight, axis=0),
            jnp.sum(hidden * hidden * pixel_weight, axis=0),
            jnp.sum(pixel_weight),
        ),
        ("gx", "gy"),
    )
    center = running / number
    spread = squares / number - center * center
    inverse = lax.rsqrt(spread + 1e-05)
    scaled = (hidden - center) * inverse
    return (scaled, inverse, number, gain * scaled + shift)


def norm_back(upstream, scaled, inverse, gain, pixel_weight, number):
    shift_grad, gain_grad = lax.psum(
        (
            jnp.sum(upstream * pixel_weight, axis=0),
            jnp.sum(upstream * scaled * pixel_weight, axis=0),
        ),
        ("gx", "gy"),
    )
    inner = (
        upstream
        - pixel_weight * (shift_grad / number)
        - pixel_weight * scaled * (gain_grad / number)
    )
    return ((gain * inverse * inner).astype(jnp.bfloat16), gain_grad, shift_grad)


def unfold(grid_in):
    edge_len = grid_in.shape[1]
    padded = jnp.pad(grid_in, ((0, 0), (1, 1), (1, 1), (0, 0)))
    pieces = [
        padded[:, tap_row : tap_row + edge_len, tap_col : tap_col + edge_len, :]
        for tap_row in range(3)
        for tap_col in range(3)
    ]
    return jnp.concatenate(pieces, axis=3).reshape(
        grid_in.shape[0] * edge_len * edge_len, 9 * grid_in.shape[3]
    )


def fold_back(columns, slot_count, edge_len, channels):
    blocks = columns.reshape(slot_count, edge_len, edge_len, 9, channels)
    running = jnp.zeros((slot_count, edge_len + 2, edge_len + 2, channels), jnp.float32)
    for tap_row in range(3):
        for tap_col in range(3):
            running = running.at[
                :, tap_row : tap_row + edge_len, tap_col : tap_col + edge_len, :
            ].add(blocks[:, :, :, 3 * tap_row + tap_col, :])
    return running[:, 1 : edge_len + 1, 1 : edge_len + 1, :].reshape(
        slot_count * edge_len * edge_len, channels
    )


def contract_rows(left_side, right_side):
    return lax.dot_general(
        left_side, right_side, (((0,), (0,)), ((), ())), preferred_element_type=jnp.float32
    )


def contract_cols(left_side, right_side):
    return lax.dot_general(
        left_side, right_side, (((1,), (1,)), ((), ())), preferred_element_type=jnp.float32
    )


def split_norms(norm_values, channels, features):
    return (
        norm_values[0:channels],
        norm_values[channels : 2 * channels],
        norm_values[2 * channels : 3 * channels],
        norm_values[3 * channels : 4 * channels],
        norm_values[4 * channels : 4 * channels + features],
        norm_values[4 * channels + features : 4 * channels + 2 * features],
    )


def per_device(views, counts, partners, w_in, w_mid, w_out, norm_params):
    slot_count, pixels, features = views.shape
    edge_len = SIDE
    row_count = slot_count * pixels
    pair_count = partners.shape[1]
    device = lax.axis_index("gx") * lax.axis_size("gy") + lax.axis_index("gy")
    filled = (jnp.arange(slot_count, dtype=jnp.int32) < counts[0]).astype(jnp.float32)
    pixel_weight = jnp.repeat(filled, pixels)[:, None]
    full_in, full_mid, full_out, full_norm = collect(w_in, w_mid, w_out, norm_params)
    channels = full_in.shape[1]
    norm_values = full_norm.astype(jnp.float32)
    gain_one, shift_one, gain_two, shift_two, gain_three, shift_three = split_norms(
        norm_values, channels, features
    )
    flat_in = views.reshape(row_count, features)
    hidden_one = jnp.dot(flat_in, full_in, preferred_element_type=jnp.float32)
    scaled_one, inverse_one, number, normed_one = normalize(
        hidden_one, gain_one, shift_one, pixel_weight
    )
    active_one = jax.nn.silu(normed_one).astype(jnp.bfloat16)
    columns = unfold(active_one.reshape(slot_count, edge_len, edge_len, channels))
    hidden_two = jnp.dot(columns, full_mid, preferred_element_type=jnp.float32)
    scaled_two, inverse_two, _, normed_two = normalize(
        hidden_two, gain_two, shift_two, pixel_weight
    )
    active_two = jax.nn.silu(normed_two).astype(jnp.bfloat16)
    hidden_three = jnp.dot(active_two, full_out, preferred_element_type=jnp.float32)
    scaled_three, inverse_three, _, normed_three = normalize(
        hidden_three, gain_three, shift_three, pixel_weight
    )
    summed = normed_three + flat_in.astype(jnp.float32)
    activated = jax.nn.silu(summed)
    pooled = jnp.sum(activated.reshape(slot_count, pixels, features), axis=1) / pixels
    factor = lax.rsqrt(jnp.mean(pooled * pooled, axis=1, keepdims=True) + 1e-06)
    embedded = (pooled * factor).astype(jnp.bfloat16)
    embedded_f = embedded.astype(jnp.float32)
    targets = partners.reshape(slot_count * pair_count)
    shard_rows = lax.all_gather(embedded, ("gx", "gy"), axis=0, tiled=True)
    positions = jnp.arange(shard_rows.shape[0], dtype=jnp.int32)
    chooser = (targets[:, None] == positions[None, :]).astype(jnp.bfloat16)
    partner_rows = jnp.dot(chooser, shard_rows, preferred_element_type=jnp.float32)
    difference = (
        embedded_f[:, None, :] - partner_rows.reshape(slot_count, pair_count, features)
    ) * filled[:, None, None]
    outgoing = (-2.0 * difference).reshape(slot_count * pair_count, features)
    positions = jnp.arange(slot_count * lax.axis_size(("gx", "gy")), dtype=jnp.int32)
    chooser = (positions[:, None] == targets[None, :]).astype(jnp.float32)
    incoming = lax.psum_scatter(
        jnp.dot(chooser, outgoing, precision=lax.Precision.HIGHEST),
        ("gx", "gy"),
        scatter_dimension=0,
        tiled=True,
    )
    objective = lax.psum(jnp.sum(difference * difference), ("gx", "gy"))
    loss_value = objective / (pair_count * features * (number / pixels))
    grad_embed = (2.0 * jnp.sum(difference, axis=1) + incoming) * filled[:, None]
    grad_pooled = (
        factor * grad_embed
        - pooled
        * (factor * factor * factor)
        * jnp.sum(pooled * grad_embed, axis=1, keepdims=True)
        / features
    )
    spread_grad = jnp.broadcast_to(
        (grad_pooled / pixels)[:, None, :], (slot_count, pixels, features)
    ).reshape(row_count, features)
    grad_summed = spread_grad * silu_slope(summed)
    back_in, back_mid, back_out, back_norm = collect(w_in, w_mid, w_out, norm_params)
    back_values = back_norm.astype(jnp.float32)
    back_gain_one, _, back_gain_two, _, back_gain_three, _ = split_norms(
        back_values, channels, features
    )
    grad_three, gain_grad_three, shift_grad_three = norm_back(
        grad_summed, scaled_three, inverse_three, back_gain_three, pixel_weight, number
    )
    out_grad = contract_rows(active_two, grad_three)
    grad_active_two = contract_cols(grad_three, back_out)
    grad_normed_two = grad_active_two * silu_slope(normed_two)
    grad_two, gain_grad_two, shift_grad_two = norm_back(
        grad_normed_two, scaled_two, inverse_two, back_gain_two, pixel_weight, number
    )
    mid_grad = contract_rows(columns, grad_two)
    grad_columns = contract_cols(grad_two, back_mid)
    grad_active_one = fold_back(grad_columns, slot_count, edge_len, channels)
    grad_normed_one = grad_active_one * silu_slope(normed_one)
    grad_one, gain_grad_one, shift_grad_one = norm_back(
        grad_normed_one, scaled_one, inverse_one, back_gain_one, pixel_weight, number
    )
    in_grad = contract_rows(flat_in, grad_one)
    views_grad = (contract_cols(grad_one, back_in) + grad_summed).reshape(
        slot_count, pixels, features
    )
    part_in, part_mid, part_out = (
        lax.psum_scatter(in_grad, "gx", scatter_dimension=0, tiled=True),
        lax.psum_scatter(mid_grad, "gx", scatter_dimension=0, tiled=True),
        lax.psum_scatter(out_grad, "gx", scatter_dimension=0, tiled=True),
    )
    own_in, own_mid, own_out = (
        lax.psum_scatter(part_in, "gy", scatter_dimension=1, tiled=True),
        lax.psum_scatter(part_mid, "gy", scatter_dimension=1, tiled=True),
        lax.psum_scatter(part_out, "gy", scatter_dimension=1, tiled=True),
    )
    norm_full = jnp.concatenate(
        [
            gain_grad_one,
            shift_grad_one,
            gain_grad_two,
            shift_grad_two,
            gain_grad_three,
            shift_grad_three,
        ]
    )
    share = norm_full.shape[0] // (lax.axis_size("gx") * lax.axis_size("gy"))
    norm_grad = lax.dynamic_slice_in_dim(norm_full, device * share, share)
    return (loss_value, views_grad, own_in, own_mid, own_out, norm_grad)


def solution(mesh):
    in_specs = (
        P(("gx", "gy"), None, None),
        P(("gx", "gy")),
        P(("gx", "gy"), None),
        P("gx", "gy"),
        P("gx", "gy"),
        P("gx", "gy"),
        P(("gx", "gy")),
    )
    out_specs = (
        P(),
        P(("gx", "gy"), None, None),
        P("gx", "gy"),
        P("gx", "gy"),
        P("gx", "gy"),
        P(("gx", "gy")),
    )
    return jax.shard_map(
        per_device, mesh=mesh, in_specs=in_specs, out_specs=out_specs, check_vma=False
    )
```

profile of v0, /device:TPU:0, one launch (start us, length us, event | category | flops | bytes accessed | tf_op | source)
XLA Modules:
  0.0 1157.9 jit_solution(8013331020981908882)
XLA Ops:
  8.0 35.6 %all_gather.37 = bf16[512,512]{0,1:T(8,128)(2,1)} all-gather(bf16[512,64]{0,1:T(8,128)(2,1)} %param.28), channel_id=1, replica_groups=mesh['gx'=4,'gy'=8] {'gy'}, dimensions={1}, use_global_device_ids=true | all-gather | bytes 589824 | tf_op jit(solution)/shard_map/all_gather | solution.py:11
  43.6 11.1 all-gather.10.cloned.1.call-done
  54.8 33.4 %all_gather.41 = bf16[128,2048]{1,0:T(8,128)(2,1)} all-gather(bf16[128,256]{1,0:T(8,128)(2,1)S(1)} %copy-done.19), channel_id=1, replica_groups=mesh['gx'=4,'gy'=8] {'gy'}, dimensions={1}, use_global_device_ids=true | all-gather | bytes 589824 | tf_op jit(solution)/shard_map/all_gather | solution.py:13
  91.2 19.7 %all-reduce.2 = bf16[1536]{0:T(1024)(128)(2,1)S(1)} all-reduce(bf16[1536]{0:T(1024)(128)(2,1)S(1)} %dynamic-update-slice.27), channel_id=1, replica_groups=mesh['gx'=4,'gy'=8] {'gy'}, use_global_device_ids=true, to_apply=%add.2 | all-reduce | flops 1536 | bytes 6144
  123.6 37.3 %all-reduce.10 = (f32[512]{0:T(512)S(1)}, f32[]{:T(128)}, f32[512]{0:T(512)S(1)}) all-reduce(f32[512]{0:T(512)S(1)} %get-tuple-element.149, f32[]{:T(128)} %broadcast_reduce_fusion, f32[512]{0:T(512)S(1)} %get-tuple-element.148), channel_id=1, replica_groups=mesh['gx'=4,'gy'=8] {'gx','gy'}, use_global_device_ids=true, to_apply=%region_5.0 | all-reduce | flops 1025 | bytes 8200 | tf_op jit(solution)/shard_map/psum | solution.py:30
  195.9 8.0 multiply_reduce_fusion.9
  203.9 42.4 %all-reduce.9 = (f32[512]{0:T(512)S(1)}, f32[512]{0:T(512)S(1)}) all-reduce(f32[512]{0:T(512)S(1)} %get-tuple-element.147, f32[512]{0:T(512)S(1)} %get-tuple-element.146), channel_id=1, replica_groups=mesh['gx'=4,'gy'=8] {'gx','gy'}, use_global_device_ids=true, to_apply=%region_9.10 | all-reduce | flops 1024 | bytes 8192 | tf_op jit(solution)/shard_map/psum | solution.py:30
  252.8 38.8 %all-reduce.8 = (f32[2048]{0:T(1024)S(1)}, f32[2048]{0:T(1024)S(1)}) all-reduce(f32[2048]{0:T(1024)S(1)} %get-tuple-element.141, f32[2048]{0:T(1024)S(1)} %get-tuple-element.140), channel_id=1, replica_groups=mesh['gx'=4,'gy'=8] {'gx','gy'}, use_global_device_ids=true, to_apply=%region_11.12 | all-reduce | flops 4096 | bytes 32768 | tf_op jit(solution)/shard_map/psum | solution.py:30
  309.7 55.6 %all-gather.16.cloned.1.call-done = bf16[32,12,2048]{2,1,0:T(8,128)(2,1)} async-done(((bf16[1,12,2048]{2,1,0:T(8,128)(2,1)}), bf16[32,12,2048]{2,1,0:T(8,128)(2,1)}) %all-gather.16.cloned.1.call-update) | async-done | bytes 1572880 | tf_op jit(solution)/shard_map/all_gather | solution.py:147
  374.3 99.8 %fusion = f32[16,2048]{1,0:T(8,128)S(1)} fusion(f32[384,2048]{1,0:T(8,128)} %fusion.3), kind=kCustom, calls=%all-reduce-scatter | all-reduce-scatter fusion | flops 1048577 | bytes 3276800
  502.0 14.8 %concatenate.60 = f32[140,2048]{1,0:T(8,128)} concatenate(f32[12,2048]{1,0:T(8,128)} %collective-permute-done.7, f32[16,2048]{1,0:T(8,128)S(1)} %collective-permute-done.6, f32[16,2048]{1,0:T(8,128)} %collective-permute-done.5, f32[16,2048]{1,0:T(8,128)} %copy-done.15, f32[16,2048]{1,0:T(8,128)} %copy-done.16, f32[16,2048]{1,0:T(8,128)} %copy-done.17, f32[16,2048]{1,0:T(8,128)} %copy-done.18, ...), dimensions={0} | concatenate | bytes 2293760
  526.7 7.3 multiply_reduce_fusion.1
  534.0 45.6 %all-reduce.7 = (f32[2048]{0:T(1024)S(1)}, f32[2048]{0:T(1024)S(1)}) all-reduce(f32[2048]{0:T(1024)S(1)} %get-tuple-element.139, f32[2048]{0:T(1024)S(1)} %get-tuple-element.138), channel_id=1, replica_groups=mesh['gx'=4,'gy'=8] {'gx','gy'}, use_global_device_ids=true, to_apply=%region_24.25 | all-reduce | flops 4096 | bytes 32768 | tf_op jit(solution)/shard_map/psum | solution.py:46
  594.6 41.5 %all-reduce.6 = (f32[512]{0:T(512)S(1)}, f32[512]{0:T(512)S(1)}) all-reduce(f32[512]{0:T(512)S(1)} %get-tuple-element.145, f32[512]{0:T(512)S(1)} %get-tuple-element.144), channel_id=1, replica_groups=mesh['gx'=4,'gy'=8] {'gx','gy'}, use_global_device_ids=true, to_apply=%region_28.29 | all-reduce | flops 1024 | bytes 8192 | tf_op jit(solution)/shard_map/psum | solution.py:46
  640.4 8.0 fusion.20
  648.4 13.9 %reshape.498 = f32[12,7,7,9,512]{4,3,2,1,0:T(8,128)} reshape(f32[588,4608]{1,0:T(8,128)} %fusion.20) | data formatting | bytes 21676032 | tf_op jit(solution)/shard_map/reshape | solution.py:75
  662.3 32.5 %fusion.17 = (f32[12,7,7,1,512]{4,3,2,1,0:T(1,128)}, f32[12,7,7,1,512]{4,3,2,1,0:T(1,128)}, f32[12,7,7,1,512]{4,3,2,1,0:T(1,128)}, f32[12,7,7,1,512]{4,3,2,1,0:T...) fusion(f32[12,7,7,9,512]{4,3,2,1,0:T(8,128)} %reshape.498), kind=kLoop, calls=%fused_computation.119 | loop fusion | bytes 21676032 | tf_op jit(solution)/shard_map/slice | solution.py:81
  770.6 39.4 %all-reduce.5 = (f32[]{:T(128)}, f32[512]{0:T(512)S(1)}, f32[512]{0:T(512)S(1)}) all-reduce(f32[]{:T(128)} %get-tuple-element.212, f32[512]{0:T(512)S(1)} %get-tuple-element.143, f32[512]{0:T(512)S(1)} %get-tuple-element.142), channel_id=1, replica_groups=mesh['gx'=4,'gy'=8] {'gx','gy'}, use_global_device_ids=true, to_apply=%region_17.18 | all-reduce | flops 1025 | bytes 8200 | tf_op jit(solution)/shard_map/psum | solution.py:163
  818.4 9.0 fusion.21
  828.2 34.0 %reduce-scatter.11.cloned.1.call-done = f32[512,512]{0,1:T(8,128)} async-done(((f32[2048,512]{0,1:T(8,128)}), f32[512,512]{0,1:T(8,128)}) %reduce-scatter.11.cloned.1.call-update) | async-done | bytes 1048592 | tf_op jit(solution)/shard_map/reduce_scatter | solution.py:203
  862.3 80.9 %reduce-scatter.15.cloned.1.call-done = f32[1152,512]{1,0:T(8,128)} async-done(((f32[4608,512]{1,0:T(8,128)}), f32[1152,512]{1,0:T(8,128)}) %reduce-scatter.15.cloned.1.call-update) | async-done | bytes 2359312 | tf_op jit(solution)/shard_map/reduce_scatter | solution.py:204
  959.9 51.2 %reduce-scatter.19.cloned.1.call-done = f32[128,256]{1,0:T(8,128)} async-done(((f32[128,2048]{1,0:T(8,128)}), f32[128,256]{1,0:T(8,128)}) %reduce-scatter.19.cloned.1.call-update) | async-done | bytes 131088 | tf_op jit(solution)/shard_map/reduce_scatter | solution.py:210
  1011.1 66.8 %reduce-scatter.13.cloned.1.call-done = f32[512,64]{0,1:T(8,128)} async-done(((f32[512,512]{0,1:T(8,128)}), f32[512,64]{0,1:T(8,128)}) %reduce-scatter.13.cloned.1.call-update) | async-done | bytes 131088 | tf_op jit(solution)/shard_map/reduce_scatter | solution.py:208
  1077.9 72.2 %reduce-scatter.21.cloned.1.call-done = f32[64,1152]{1,0:T(8,128)} async-done(((f32[512,1152]{1,0:T(8,128)}), f32[64,1152]{1,0:T(8,128)}) %reduce-scatter.21.cloned.1.call-update) | async-done | bytes 294928
  (220 shorter events, 240.6 us)
Async XLA Ops:
  7.2 47.7 %copy-start.19 = (bf16[128,256]{1,0:T(8,128)(2,1)S(1)}, bf16[128,256]{1,0:T(8,128)(2,1)}, u32[]{:S(2)}) copy-start(bf16[128,256]{1,0:T(8,128)(2,1)} %param.30) | copy-start | bytes 196612
  7.2 47.6 %all-gather.10.cloned.1.call-start = ((), (), s32[]{:S(2)}) async-start(), calls=%async_computation.7 | async-start | bytes 1327104 | tf_op jit(solution)/shard_map/all_gather | solution.py:12
  7.9 110.8 %all-gather.8.cloned.1.call-start = ((), (), s32[]{:S(2)}) async-start(), calls=%async_computation.6 | async-start | bytes 2621440 | tf_op jit(solution)/shard_map/all_gather | solution.py:17
  43.5 46.1 %copy-start.35 = (u32[32]{0:T(128)S(1)}, u32[32]{0:T(128)}, u32[]{:S(2)}) copy-start(u32[32]{0:T(128)} %constant.326) | copy-start | bytes 388
  43.5 47.4 %copy-start.34 = (bf16[192]{0:T(256)(128)(2,1)S(1)}, bf16[192]{0:T(256)(128)(2,1)}, u32[]{:S(2)}) copy-start(bf16[192]{0:T(256)(128)(2,1)} %param.31) | copy-start | bytes 1156
  43.6 152.3 %all-gather.12.cloned.1.call-start = ((), (), s32[]{:S(2)}) async-start(), calls=%async_computation.8 | async-start | bytes 5898240 | tf_op jit(solution)/shard_map/all_gather | solution.py:18
  54.8 192.2 %all-gather.14.cloned.1.call-start = ((), (), s32[]{:S(2)}) async-start(), calls=%async_computation.9 | async-start | bytes 2621440 | tf_op jit(solution)/shard_map/all_gather | solution.py:19
  88.2 277.0 %all-gather.16.cloned.1.call-start = ((), (), s32[]{:S(2)}) async-start(), calls=%async_computation.15 | async-start | bytes 2162688 | tf_op jit(solution)/shard_map/all_gather | solution.py:147
  118.6 408.1 %copy-start = (bf16[588,2048]{1,0:T(8,128)(2,1)}, bf16[588,2048]{1,0:T(8,128)(2,1)S(1)}, u32[]{:S(2)}) copy-start(bf16[588,2048]{1,0:T(8,128)(2,1)S(1)} %reshape.493) | copy-start | bytes 7225348
  308.2 519.3 %reduce-scatter.17.cloned.1.call-start = ((), (), s32[]{:S(2)}) async-start(), calls=%async_computation.13 | async-start | bytes 5242880 | tf_op jit(solution)/shard_map/reduce_scatter | solution.py:205
  474.1 18.5 %collective-permute-start.6 = (f32[16,2048]{1,0:T(8,128)S(1)}, f32[16,2048]{1,0:T(8,128)S(1)}, u32[]{:S(2)}, u32[]{:S(2)}) collective-permute-start(f32[16,2048]{1,0:T(8,128)S(1)} %fusion), channel_id=1, source_target_pairs={{0,7},{1,8},{2,9},{3,10},{4,11},{5,12},{6,13},{7,14},{8,15},{9,16}... | collective-permute-start | bytes 393224
  477.4 17.8 %collective-permute-start.5 = (f32[16,2048]{1,0:T(8,128)S(1)}, f32[16,2048]{1,0:T(8,128)}, u32[]{:S(2)}, u32[]{:S(2)}) collective-permute-start(f32[16,2048]{1,0:T(8,128)S(1)} %fusion), channel_id=1, source_target_pairs={{0,6},{1,7},{2,8},{3,9},{4,10},{5,11},{6,12},{7,13},{8,14},{9,15},... | collective-permute-start | bytes 393224
  481.0 9.7 collective-permute-start.7
  484.1 15.8 %collective-permute-start.4 = (f32[16,2048]{1,0:T(8,128)S(1)}, f32[16,2048]{1,0:T(8,128)S(1)}, u32[]{:S(2)}, u32[]{:S(2)}) collective-permute-start(f32[16,2048]{1,0:T(8,128)S(1)} %fusion), channel_id=1, source_target_pairs={{0,5},{1,6},{2,7},{3,8},{4,9},{5,10},{6,11},{7,12},{8,13},{9,14},{... | collective-permute-start | bytes 393224
  486.9 13.0 %collective-permute-start.3 = (f32[16,2048]{1,0:T(8,128)S(1)}, f32[16,2048]{1,0:T(8,128)S(1)}, u32[]{:S(2)}, u32[]{:S(2)}) collective-permute-start(f32[16,2048]{1,0:T(8,128)S(1)} %fusion), channel_id=1, source_target_pairs={{0,4},{1,5},{2,6},{3,7},{4,8},{5,9},{6,10},{7,11},{8,12},{9,13},{1... | collective-permute-start | bytes 393224
  490.6 9.2 collective-permute-start.2
  492.6 7.3 collective-permute-start.1
  495.1 6.8 collective-permute-start
  589.7 272.5 %reduce-scatter.11.cloned.1.call-start = ((), (), s32[]{:S(2)}) async-start(), calls=%async_computation.10 | async-start | bytes 5242880 | tf_op jit(solution)/shard_map/reduce_scatter | solution.py:203
  768.9 42.5 %copy-start.30 = (f32[512]{0:T(512)S(1)}, f32[512]{0:T(512)}, u32[]{:S(2)}) copy-start(f32[512]{0:T(512)} %get-tuple-element.164) | copy-start | bytes 6148
  817.4 125.8 %reduce-scatter.15.cloned.1.call-start = ((), (), s32[]{:S(2)}) async-start(), calls=%async_computation.12 | async-start | bytes 11796480 | tf_op jit(solution)/shard_map/reduce_scatter | solution.py:204
  827.5 183.6 %reduce-scatter.19.cloned.1.call-start = ((), (), s32[]{:S(2)}) async-start(), calls=%async_computation.14 | async-start | bytes 1179648 | tf_op jit(solution)/shard_map/reduce_scatter | solution.py:210
  828.2 249.7 %reduce-scatter.13.cloned.1.call-start = ((), (), s32[]{:S(2)}) async-start(), calls=%async_computation.11 | async-start | bytes 1179648 | tf_op jit(solution)/shard_map/reduce_scatter | solution.py:208
  862.3 287.8 %reduce-scatter.21.cloned.1.call-start = ((), (), s32[]{:S(2)}) async-start(), calls=%async_computation.16 | async-start | bytes 2654208
  (31 other events, 153.7 us)
Sparse Core Ops, SparseCore 0:
  10.2 44.5 all-gather.9
  56.3 21.7 all-gather.7
  79.7 37.5 all-gather.11
  118.7 23.1 all-gather.13
  308.3 56.8 all-gather.15
  589.8 44.9 reduce-scatter.16
  817.5 44.6 reduce-scatter.10
  864.8 78.3 reduce-scatter.14
  947.2 63.8 reduce-scatter.18
  1015.3 62.5 reduce-scatter.12
  1081.9 68.0 reduce-scatter.20
where the time goes:
time: 1170 us; the launch traced here: 1160 us
  blocking collectives  439 us (38%)
  waiting for transfers between devices  374 us (32%)
  local copies, waits for them, and re-layouts  176 us (15%)
  other arithmetic  66.4 us (6%)
  matrix products  60.6 us (5%)
  starting transfers between devices  23.5 us (2%)
  between operations  18.5 us (2%)
    unnamed x2, blocking collectives  119 us
    psum x3, blocking collectives, normalize(): lax.psum((jnp.sum(hidden * pixel_weight, axis=0), jnp.sum(hidden * hidden...  118 us
    psum x2, blocking collectives, norm_back(): lax.psum((jnp.sum(upstream * pixel_weight, axis=0), jnp.sum(upstream * sc...  87.1 us
    reduce_scatter x1, waiting for transfers between devices, per_device(): lax.psum_scatter(mid_grad, 'gx', scatter_dimension=0, tiled=True)  80.9 us
    unnamed x20, waiting for transfers between devices  74.4 us
    reduce_scatter x1, waiting for transfers between devices, per_device(): lax.psum_scatter(part_in, 'gy', scatter_dimension=1, tiled=True)  66.8 us
    all_gather x1, waiting for transfers between devices, per_device(): shard_rows = lax.all_gather(embedded, ('gx', 'gy'), axis=0, tiled=True)  55.6 us
    reduce_scatter x1, waiting for transfers between devices, per_device(): lax.psum_scatter(part_out, 'gy', scatter_dimension=1, tiled=True)  51.2 us
  transfers between devices with their start and end apart: 19, of which 8 were waited for; matrix products, arithmetic and copies ran while one was open for 19% of the time, Pallas kernels for 0%

commit v1 on v0

--- a/solution.py
+++ b/solution.py
@@ -44,11 +44,14 @@
 
 def norm_back(upstream, scaled, inverse, gain, pixel_weight, number):
     shift_grad, gain_grad = lax.psum(
-        (
-            jnp.sum(upstream * pixel_weight, axis=0),
-            jnp.sum(upstream * scaled * pixel_weight, axis=0),
+        lax.psum(
+            (
+                jnp.sum(upstream * pixel_weight, axis=0),
+                jnp.sum(upstream * scaled * pixel_weight, axis=0),
+            ),
+            "gy",
         ),
-        ("gx", "gy"),
+        "gx",
     )
     inner = (
         upstream

time: 1170 us -> 1140 us (0.974)
  waiting for transfers between devices: 374 us -> 332 us
    reduce_scatter x1, waiting for transfers between devices: 51.2 us -> 11.6 us  [per_device(): lax.psum_scatter(part_out, 'gy', scatter_dimension=1, tiled=True)]
    psum x0 -> x3, blocking collectives: none -> 22.8 us  [norm_back(): lax.psum(lax.psum((jnp.sum(upstream * pixel_weight, axis=0), jnp.sum(upst...]
    psum x2 -> x3, blocking collectives: 87.1 us -> 75 us  [norm_back(): lax.psum((jnp.sum(upstream * pixel_weight, axis=0), jnp.sum(upstream * sc...]
  transfers between devices with their start and end apart: 19 -> 19, of which waited for: 8 -> 8; matrix products, arithmetic and copies ran while one was open for 19% -> 20% of each run, Pallas kernels for 0% -> 0%
where the time goes in v1:
time: 1140 us; the launch traced here: 1130 us
  blocking collectives  449 us (39%)
  waiting for transfers between devices  332 us (29%)
  local copies, waits for them, and re-layouts  176 us (15%)
  other arithmetic  66.2 us (6%)
  matrix products  60.7 us (5%)
  starting transfers between devices  26.5 us (2%)
  between operations  18.5 us (2%)
    unnamed x2, blocking collectives  118 us
    psum x3, blocking collectives, normalize(): lax.psum((jnp.sum(hidden * pixel_weight, axis=0), jnp.sum(hidden * hidden...  118 us
    reduce_scatter x1, waiting for transfers between devices, per_device(): lax.psum_scatter(mid_grad, 'gx', scatter_dimension=0, tiled=True)  81 us
    psum x3, blocking collectives, norm_back(): lax.psum((jnp.sum(upstream * pixel_weight, axis=0), jnp.sum(upstream * sc...  75 us
    unnamed x20, waiting for transfers between devices  74.3 us
    reduce_scatter x1, waiting for transfers between devices, per_device(): lax.psum_scatter(part_in, 'gy', scatter_dimension=1, tiled=True)  66.6 us
    all_gather x1, waiting for transfers between devices, per_device(): shard_rows = lax.all_gather(embedded, ('gx', 'gy'), axis=0, tiled=True)  55.6 us
    scatter-add x9, local copies, waits for them, and re-layouts, fold_back(): running = running.at[:, tap_row:tap_row + edge_len, tap_col:tap_col + edg...  45.6 us
  transfers between devices with their start and end apart: 19, of which 8 were waited for; matrix products, arithmetic and copies ran while one was open for 20% of the time, Pallas kernels for 0%

profile of v1, /device:TPU:0, one launch (start us, length us, event | category | flops | bytes accessed | tf_op | source)
XLA Modules:
  0.0 1128.4 jit_solution(13304149849738259498)
XLA Ops:
  8.0 35.6 %all_gather.37 = bf16[512,512]{0,1:T(8,128)(2,1)} all-gather(bf16[512,64]{0,1:T(8,128)(2,1)} %param.28), channel_id=1, replica_groups=mesh['gx'=4,'gy'=8] {'gy'}, dimensions={1}, use_global_device_ids=true | all-gather | bytes 589824 | tf_op jit(solution)/shard_map/all_gather | solution.py:11
  43.6 11.1 all-gather.10.cloned.1.call-done
  54.8 33.4 %all_gather.41 = bf16[128,2048]{1,0:T(8,128)(2,1)} all-gather(bf16[128,256]{1,0:T(8,128)(2,1)S(1)} %copy-done.19), channel_id=1, replica_groups=mesh['gx'=4,'gy'=8] {'gy'}, dimensions={1}, use_global_device_ids=true | all-gather | bytes 589824 | tf_op jit(solution)/shard_map/all_gather | solution.py:13
  91.2 19.7 %all-reduce.2 = bf16[1536]{0:T(1024)(128)(2,1)S(1)} all-reduce(bf16[1536]{0:T(1024)(128)(2,1)S(1)} %dynamic-update-slice.27), channel_id=1, replica_groups=mesh['gx'=4,'gy'=8] {'gy'}, use_global_device_ids=true, to_apply=%add.2 | all-reduce | flops 1536 | bytes 6144
  123.6 37.3 %all-reduce.7 = (f32[512]{0:T(512)S(1)}, f32[]{:T(128)}, f32[512]{0:T(512)S(1)}) all-reduce(f32[512]{0:T(512)S(1)} %get-tuple-element.149, f32[]{:T(128)} %broadcast_reduce_fusion, f32[512]{0:T(512)S(1)} %get-tuple-element.148), channel_id=1, replica_groups=mesh['gx'=4,'gy'=8] {'gx','gy'}, use_global_device_ids=true, to_apply=%region_5.0 | all-reduce | flops 1025 | bytes 8200 | tf_op jit(solution)/shard_map/psum | solution.py:30
  195.9 8.0 multiply_reduce_fusion.9
  203.9 42.3 %all-reduce.6 = (f32[512]{0:T(512)S(1)}, f32[512]{0:T(512)S(1)}) all-reduce(f32[512]{0:T(512)S(1)} %get-tuple-element.147, f32[512]{0:T(512)S(1)} %get-tuple-element.146), channel_id=1, replica_groups=mesh['gx'=4,'gy'=8] {'gx','gy'}, use_global_device_ids=true, to_apply=%region_9.10 | all-reduce | flops 1024 | bytes 8192 | tf_op jit(solution)/shard_map/psum | solution.py:30
  252.8 38.8 %all-reduce.5 = (f32[2048]{0:T(1024)S(1)}, f32[2048]{0:T(1024)S(1)}) all-reduce(f32[2048]{0:T(1024)S(1)} %get-tuple-element.141, f32[2048]{0:T(1024)S(1)} %get-tuple-element.140), channel_id=1, replica_groups=mesh['gx'=4,'gy'=8] {'gx','gy'}, use_global_device_ids=true, to_apply=%region_11.12 | all-reduce | flops 4096 | bytes 32768 | tf_op jit(solution)/shard_map/psum | solution.py:30
  309.7 55.6 %all-gather.16.cloned.1.call-done = bf16[32,12,2048]{2,1,0:T(8,128)(2,1)} async-done(((bf16[1,12,2048]{2,1,0:T(8,128)(2,1)}), bf16[32,12,2048]{2,1,0:T(8,128)(2,1)}) %all-gather.16.cloned.1.call-update) | async-done | bytes 1572880 | tf_op jit(solution)/shard_map/all_gather | solution.py:150
  374.3 98.8 %fusion = f32[16,2048]{1,0:T(8,128)S(1)} fusion(f32[384,2048]{1,0:T(8,128)} %fusion.3), kind=kCustom, calls=%all-reduce-scatter | all-reduce-scatter fusion | flops 1048577 | bytes 3276800
  503.9 14.8 %concatenate.60 = f32[140,2048]{1,0:T(8,128)} concatenate(f32[12,2048]{1,0:T(8,128)} %collective-permute-done.7, f32[16,2048]{1,0:T(8,128)S(1)} %collective-permute-done.6, f32[16,2048]{1,0:T(8,128)} %collective-permute-done.5, f32[16,2048]{1,0:T(8,128)} %copy-done.15, f32[16,2048]{1,0:T(8,128)} %copy-done.16, f32[16,2048]{1,0:T(8,128)} %copy-done.17, f32[16,2048]{1,0:T(8,128)} %copy-done.18, ...), dimensions={0} | concatenate | bytes 2293760
  535.9 38.6 %all-reduce.10 = (f32[2048]{0:T(1024)S(1)}, f32[2048]{0:T(1024)S(1)}) all-reduce(f32[2048]{0:T(1024)S(1)} %get-tuple-element.139, f32[2048]{0:T(1024)S(1)} %get-tuple-element.138), channel_id=1, replica_groups=mesh['gx'=4,'gy'=8] {'gy'}, use_global_device_ids=true, to_apply=%region_25.26 | all-reduce | flops 4096 | bytes 32768 | tf_op jit(solution)/shard_map/psum | solution.py:47
  574.5 10.6 all-reduce.13
  600.1 17.1 %all-reduce.9 = (f32[512]{0:T(512)S(1)}, f32[512]{0:T(512)S(1)}) all-reduce(f32[512]{0:T(512)S(1)} %get-tuple-element.145, f32[512]{0:T(512)S(1)} %get-tuple-element.144), channel_id=1, replica_groups=mesh['gx'=4,'gy'=8] {'gy'}, use_global_device_ids=true, to_apply=%region_31.32 | all-reduce | flops 1024 | bytes 8192 | tf_op jit(solution)/shard_map/psum | solution.py:47
  636.0 14.0 %reshape.498 = f32[12,7,7,9,512]{4,3,2,1,0:T(8,128)} reshape(f32[588,4608]{1,0:T(8,128)} %fusion.20) | data formatting | bytes 21676032 | tf_op jit(solution)/shard_map/reshape | solution.py:78
  649.9 32.4 %fusion.17 = (f32[12,7,7,1,512]{4,3,2,1,0:T(1,128)}, f32[12,7,7,1,512]{4,3,2,1,0:T(1,128)}, f32[12,7,7,1,512]{4,3,2,1,0:T(1,128)}, f32[12,7,7,1,512]{4,3,2,1,0:T...) fusion(f32[12,7,7,9,512]{4,3,2,1,0:T(8,128)} %reshape.498), kind=kLoop, calls=%fused_computation.119 | loop fusion | bytes 21676032 | tf_op jit(solution)/shard_map/slice | solution.py:84
  757.8 19.3 %all-reduce.8 = (f32[512]{0:T(512)S(1)}, f32[512]{0:T(512)S(1)}) all-reduce(f32[512]{0:T(512)S(1)} %get-tuple-element.143, f32[512]{0:T(512)S(1)} %get-tuple-element.142), channel_id=1, replica_groups=mesh['gx'=4,'gy'=8] {'gy'}, use_global_device_ids=true, to_apply=%region_38.39 | all-reduce | flops 1024 | bytes 8192 | tf_op jit(solution)/shard_map/psum | solution.py:47
  791.2 9.1 fusion.21
  801.1 31.7 %reduce-scatter.11.cloned.1.call-done = f32[512,512]{0,1:T(8,128)} async-done(((f32[2048,512]{0,1:T(8,128)}), f32[512,512]{0,1:T(8,128)}) %reduce-scatter.11.cloned.1.call-update) | async-done | bytes 1048592 | tf_op jit(solution)/shard_map/reduce_scatter | solution.py:206
  832.8 81.0 %reduce-scatter.15.cloned.1.call-done = f32[1152,512]{1,0:T(8,128)} async-done(((f32[4608,512]{1,0:T(8,128)}), f32[1152,512]{1,0:T(8,128)}) %reduce-scatter.15.cloned.1.call-update) | async-done | bytes 2359312 | tf_op jit(solution)/shard_map/reduce_scatter | solution.py:207
  917.6 39.9 %psum.153 = f32[]{:T(128)} all-reduce(f32[]{:T(128)} %get-tuple-element.217), channel_id=1, replica_groups=mesh['gx'=4,'gy'=8] {'gx','gy'}, use_global_device_ids=true, to_apply=%region_17.18 | all-reduce | flops 1 | bytes 8 | tf_op jit(solution)/shard_map/psum | solution.py:166
  970.3 11.6 %reduce-scatter.19.cloned.1.call-done = f32[128,256]{1,0:T(8,128)} async-done(((f32[128,2048]{1,0:T(8,128)}), f32[128,256]{1,0:T(8,128)}) %reduce-scatter.19.cloned.1.call-update) | async-done | bytes 131088 | tf_op jit(solution)/shard_map/reduce_scatter | solution.py:213
  981.8 66.6 %reduce-scatter.13.cloned.1.call-done = f32[512,64]{0,1:T(8,128)} async-done(((f32[512,512]{0,1:T(8,128)}), f32[512,64]{0,1:T(8,128)}) %reduce-scatter.13.cloned.1.call-update) | async-done | bytes 131088 | tf_op jit(solution)/shard_map/reduce_scatter | solution.py:211
  1048.4 72.2 %reduce-scatter.21.cloned.1.call-done = f32[64,1152]{1,0:T(8,128)} async-done(((f32[512,1152]{1,0:T(8,128)}), f32[64,1152]{1,0:T(8,128)}) %reduce-scatter.21.cloned.1.call-update) | async-done | bytes 294928
  (224 shorter events, 270.6 us)
Async XLA Ops:
  7.2 47.7 %copy-start.19 = (bf16[128,256]{1,0:T(8,128)(2,1)S(1)}, bf16[128,256]{1,0:T(8,128)(2,1)}, u32[]{:S(2)}) copy-start(bf16[128,256]{1,0:T(8,128)(2,1)} %param.30) | copy-start | bytes 196612
  7.2 47.6 %all-gather.10.cloned.1.call-start = ((), (), s32[]{:S(2)}) async-start(), calls=%async_computation.7 | async-start | bytes 1327104 | tf_op jit(solution)/shard_map/all_gather | solution.py:12
  7.9 110.8 %all-gather.8.cloned.1.call-start = ((), (), s32[]{:S(2)}) async-start(), calls=%async_computation.6 | async-start | bytes 2621440 | tf_op jit(solution)/shard_map/all_gather | solution.py:17
  43.5 46.1 %copy-start.35 = (u32[32]{0:T(128)S(1)}, u32[32]{0:T(128)}, u32[]{:S(2)}) copy-start(u32[32]{0:T(128)} %constant.326) | copy-start | bytes 388
  43.5 47.4 %copy-start.34 = (bf16[192]{0:T(256)(128)(2,1)S(1)}, bf16[192]{0:T(256)(128)(2,1)}, u32[]{:S(2)}) copy-start(bf16[192]{0:T(256)(128)(2,1)} %param.31) | copy-start | bytes 1156
  43.6 152.4 %all-gather.12.cloned.1.call-start = ((), (), s32[]{:S(2)}) async-start(), calls=%async_computation.8 | async-start | bytes 5898240 | tf_op jit(solution)/shard_map/all_gather | solution.py:18
  54.8 192.2 %all-gather.14.cloned.1.call-start = ((), (), s32[]{:S(2)}) async-start(), calls=%async_computation.9 | async-start | bytes 2621440 | tf_op jit(solution)/shard_map/all_gather | solution.py:19
  88.2 277.0 %all-gather.16.cloned.1.call-start = ((), (), s32[]{:S(2)}) async-start(), calls=%async_computation.15 | async-start | bytes 2162688 | tf_op jit(solution)/shard_map/all_gather | solution.py:150
  118.6 410.0 %copy-start = (bf16[588,2048]{1,0:T(8,128)(2,1)}, bf16[588,2048]{1,0:T(8,128)(2,1)S(1)}, u32[]{:S(2)}) copy-start(bf16[588,2048]{1,0:T(8,128)(2,1)S(1)} %reshape.493) | copy-start | bytes 7225348
  162.1 28.9 %copy-start.20 = (f32[512]{0:T(512)}, f32[512]{0:T(512)S(1)}, u32[]{:S(2)}) copy-start(f32[512]{0:T(512)S(1)} %get-tuple-element.203) | copy-start | bytes 6148
  308.2 492.1 %reduce-scatter.17.cloned.1.call-start = ((), (), s32[]{:S(2)}) async-start(), calls=%async_computation.13 | async-start | bytes 5242880 | tf_op jit(solution)/shard_map/reduce_scatter | solution.py:208
  473.2 20.3 %collective-permute-start.6 = (f32[16,2048]{1,0:T(8,128)S(1)}, f32[16,2048]{1,0:T(8,128)S(1)}, u32[]{:S(2)}, u32[]{:S(2)}) collective-permute-start(f32[16,2048]{1,0:T(8,128)S(1)} %fusion), channel_id=1, source_target_pairs={{0,7},{1,8},{2,9},{3,10},{4,11},{5,12},{6,13},{7,14},{8,15},{9,16}... | collective-permute-start | bytes 393224
  480.3 16.8 %collective-permute-start.5 = (f32[16,2048]{1,0:T(8,128)S(1)}, f32[16,2048]{1,0:T(8,128)}, u32[]{:S(2)}, u32[]{:S(2)}) collective-permute-start(f32[16,2048]{1,0:T(8,128)S(1)} %fusion), channel_id=1, source_target_pairs={{0,6},{1,7},{2,8},{3,9},{4,10},{5,11},{6,12},{7,13},{8,14},{9,15},... | collective-permute-start | bytes 393224
  483.5 8.7 collective-permute-start.7
  486.2 15.7 %collective-permute-start.4 = (f32[16,2048]{1,0:T(8,128)S(1)}, f32[16,2048]{1,0:T(8,128)S(1)}, u32[]{:S(2)}, u32[]{:S(2)}) collective-permute-start(f32[16,2048]{1,0:T(8,128)S(1)} %fusion), channel_id=1, source_target_pairs={{0,5},{1,6},{2,7},{3,8},{4,9},{5,10},{6,11},{7,12},{8,13},{9,14},{... | collective-permute-start | bytes 393224
  488.1 13.8 %collective-permute-start.3 = (f32[16,2048]{1,0:T(8,128)S(1)}, f32[16,2048]{1,0:T(8,128)S(1)}, u32[]{:S(2)}, u32[]{:S(2)}) collective-permute-start(f32[16,2048]{1,0:T(8,128)S(1)} %fusion), channel_id=1, source_target_pairs={{0,4},{1,5},{2,6},{3,7},{4,8},{5,9},{6,10},{7,11},{8,12},{9,13},{1... | collective-permute-start | bytes 393224
  492.2 9.7 collective-permute-start.2
  493.5 8.4 collective-permute-start.1
  497.1 6.8 collective-permute-start
  595.2 237.6 %reduce-scatter.11.cloned.1.call-start = ((), (), s32[]{:S(2)}) async-start(), calls=%async_computation.10 | async-start | bytes 5242880 | tf_op jit(solution)/shard_map/reduce_scatter | solution.py:206
  790.1 123.7 %reduce-scatter.15.cloned.1.call-start = ((), (), s32[]{:S(2)}) async-start(), calls=%async_computation.12 | async-start | bytes 11796480 | tf_op jit(solution)/shard_map/reduce_scatter | solution.py:207
  800.3 181.5 %reduce-scatter.19.cloned.1.call-start = ((), (), s32[]{:S(2)}) async-start(), calls=%async_computation.14 | async-start | bytes 1179648 | tf_op jit(solution)/shard_map/reduce_scatter | solution.py:213
  801.0 247.4 %reduce-scatter.13.cloned.1.call-start = ((), (), s32[]{:S(2)}) async-start(), calls=%async_computation.11 | async-start | bytes 1179648 | tf_op jit(solution)/shard_map/reduce_scatter | solution.py:211
  832.8 287.8 %reduce-scatter.21.cloned.1.call-start = ((), (), s32[]{:S(2)}) async-start(), calls=%async_computation.16 | async-start | bytes 2654208
  (31 other events, 135.6 us)
Sparse Core Ops, SparseCore 0:
  10.2 44.5 all-gather.9
  56.3 21.7 all-gather.7
  79.7 37.5 all-gather.11
  118.7 23.1 all-gather.13
  308.3 56.8 all-gather.15
  595.3 42.6 reduce-scatter.16
  790.2 42.4 reduce-scatter.10
  835.3 78.4 reduce-scatter.14
  917.8 64.0 reduce-scatter.18
  986.0 62.3 reduce-scatter.12
  1052.5 68.0 reduce-scatter.20
